TPU v7x, 512 devices: a whole 4x4x16 slice. The times are simulated.
512 devices in a mesh: shot: 16 (over z_lo, core), px: 8 (over y, z_hi), py: 4 (over x).
Axes of the slice: x: 4, y: 4, z: 16 (z_hi: 2, z_lo: 8; z = z_hi * 8 + z_lo), core: 2. Of those that a mesh axis runs over, the one named last changes fastest.
Arguments:
- fwd_before: float32 [16, 32, 192, 512], P('shot', None, 'px', 'py'), may hold values from -6 to 6
- fwd_now: float32 [16, 32, 192, 512], P('shot', None, 'px', 'py'), may hold values from -6 to 6
- adj_after: float32 [16, 32, 192, 512], P('shot', None, 'px', 'py'), may hold values from -6 to 6
- adj_now: float32 [16, 32, 192, 512], P('shot', None, 'px', 'py'), may hold values from -8 to 8
- speed: float32 [32, 192, 512], P(None, 'px', 'py'), may hold values from 1.5 to 4.5
- src_pos: int32 [16, 8, 3], P('shot'), may hold values from 0 to 511, as said below
- src_amp: float32 [16, 2, 8], P('shot'), may hold values from -12 to 12
- rec_pos: int32 [16, 256, 3], P('shot'), may hold values from 0 to 511, as said below
- observed: float32 [16, 2, 256], P('shot'), may hold values from -6 to 6
- rate: float32 [1], replicated, may hold values from 0.05 to 0.2
Outputs:
- fwd_mid: float32 [16, 32, 192, 512], P('shot', None, 'px', 'py')
- fwd_last: float32 [16, 32, 192, 512], P('shot', None, 'px', 'py')
- adj_mid: float32 [16, 32, 192, 512], P('shot', None, 'px', 'py')
- adj_last: float32 [16, 32, 192, 512], P('shot', None, 'px', 'py')
- new_speed: float32 [32, 192, 512], P(None, 'px', 'py')
- gradient: float32 [32, 192, 512], P('shot', 'px', 'py')
Inputs may be any that keep to these rules, and one draw needn't show every extreme that they name: `src_pos`: each row holds a depth index below 32, a first index below 192 and a second index below 512; cells may repeat. `rec_pos`: each row holds a depth index below 32, a first index below 192 and a second index below 512; cells may repeat.
All inputs are finite; a program needn't handle non-finite values.
Results may differ from a plain program's by a relative error of at most 0.00002.
Values sent between devices are 32-bit elements; how exact they have to be, the bound alone decides.
A program may use at most 64 MiB of HBM per device.

v0:
```python
import jax
import jax.numpy as jnp
from jax import lax
from jax.sharding import PartitionSpec as P

STENCIL_WEIGHTS = (-205.0 / 72.0, 1.6, -0.2, 8.0 / 315.0, -1.0 / 560.0)
TIME_FACTOR = 0.009


def extended_2(cells, sides, width):
    for axis, dim in sides:
        count = lax.axis_size(axis)
        ends = count - 1
        head = lax.slice_in_dim(cells, 0, width, axis=dim)
        tail = lax.slice_in_dim(cells, cells.shape[dim] - width, cells.shape[dim], axis=dim)
        cells = jnp.concatenate(
            [
                lax.ppermute(tail, axis, [(i, (i + 1) % count) for i in range(ends)]),
                cells,
                lax.ppermute(head, axis, [((i + 1) % count, i) for i in range(ends)]),
            ],
            axis=dim,
        )
    return cells


def stencil(extended):
    depth = extended.shape[0]
    rows = extended.shape[1] - 8
    cols = extended.shape[2] - 8
    padded = jnp.pad(extended, ((4, 4), (0, 0), (0, 0)))
    total = 3.0 * STENCIL_WEIGHTS[0] * padded[4 : 4 + depth, 4 : 4 + rows, 4 : 4 + cols]
    for reach in range(1, 5):
        near = (
            padded[4 + reach : 4 + reach + depth, 4 : 4 + rows, 4 : 4 + cols]
            + padded[4 - reach : 4 - reach + depth, 4 : 4 + rows, 4 : 4 + cols]
        )
        near = (
            near
            + padded[4 : 4 + depth, 4 + reach : 4 + reach + rows, 4 : 4 + cols]
            + padded[4 : 4 + depth, 4 - reach : 4 - reach + rows, 4 : 4 + cols]
        )
        near = (
            near
            + padded[4 : 4 + depth, 4 : 4 + rows, 4 + reach : 4 + reach + cols]
            + padded[4 : 4 + depth, 4 : 4 + rows, 4 - reach : 4 - reach + cols]
        )
        total = total + STENCIL_WEIGHTS[reach] * near
    return total


def laplace(field):
    extended = extended_2(field, (("px", 1), ("py", 2)), 4)
    return stencil(extended)


def local(
    fwd_before, fwd_now, adj_after, adj_now, speed, src_pos, src_amp, rec_pos, observed, rate
):
    before = fwd_before[0]
    current = fwd_now[0]
    after = adj_after[0]
    adjoint = adj_now[0]
    depth, rows, cols = current.shape
    first_start = lax.axis_index("px") * rows
    second_start = lax.axis_index("py") * cols
    coef = TIME_FACTOR * speed * speed

    def locate(points):
        first = points[:, 1] - first_start
        second = points[:, 2] - second_start
        owned = (first >= 0) & (first < rows) & (second >= 0) & (second < cols)
        return (points[:, 0], jnp.clip(first, 0, rows - 1), jnp.clip(second, 0, cols - 1), owned)

    src_depth, src_first, src_second, src_owned = locate(src_pos[0])
    rec_depth, rec_first, rec_second, rec_owned = locate(rec_pos[0])
    amplitudes = src_amp[0]
    data = observed[0]

    def add_sources(field, values):
        return field.at[src_depth, src_first, src_second].add(jnp.where(src_owned, values, 0.0))

    def add_receivers(field, values):
        return field.at[rec_depth, rec_first, rec_second].add(jnp.where(rec_owned, values, 0.0))

    lap_one = laplace(current)
    middle = add_sources(2.0 * current - before + coef * lap_one, amplitudes[0])
    lap_two = laplace(middle)
    final = add_sources(2.0 * middle - current + coef * lap_two, amplitudes[1])
    miss_two = middle[rec_depth, rec_first, rec_second] - data[0]
    miss_three = final[rec_depth, rec_first, rec_second] - data[1]
    adj_middle = add_receivers(2.0 * adjoint - after + laplace(coef * adjoint), miss_three)
    adj_final = add_receivers(2.0 * adj_middle - adjoint + laplace(coef * adj_middle), miss_two)
    image = adj_middle * lap_one + adjoint * lap_two
    term = 2.0 * TIME_FACTOR * speed * image
    summed = lax.psum_scatter(term, "shot", scatter_dimension=0, tiled=True)
    slab_rows = summed.shape[0]
    own_slab = lax.dynamic_slice_in_dim(speed, lax.axis_index("shot") * slab_rows, slab_rows, 0)
    new_slab = own_slab - rate[0] * summed
    new_speed = lax.all_gather(new_slab, "shot", axis=0, tiled=True)
    return (middle[None], final[None], adj_middle[None], adj_final[None], new_speed, summed)


def solution(mesh):
    placed = (
        P("shot", None, "px", "py"),
        P("shot", None, "px", "py"),
        P("shot", None, "px", "py"),
        P("shot", None, "px", "py"),
        P(None, "px", "py"),
        P("shot", None, None),
        P("shot", None, None),
        P("shot", None, None),
        P("shot", None, None),
        P(),
    )
    return jax.shard_map(
        local,
        mesh=mesh,
        in_specs=placed,
        out_specs=(
            P("shot", None, "px", "py"),
            P("shot", None, "px", "py"),
            P("shot", None, "px", "py"),
            P("shot", None, "px", "py"),
            P(None, "px", "py"),
            P("shot", "px", "py"),
        ),
        check_vma=False,
    )
```

profile of v0, /device:TPU:1, one launch (start us, length us, event | category | flops | bytes accessed | tf_op | source)
XLA Modules:
  0.0 309.6 jit_solution(18226822303002385530)
XLA Ops:
  7.3 1.0 fusion.127
  8.3 1.3 collective-permute-start.1
  9.6 16.9 %collective-permute-start = (f32[32,4,128]{2,1,0:T(4,128)S(1)}, f32[32,4,128]{2,1,0:T(4,128)S(1)}, u32[]{:S(2)}, u32[]{:S(2)}) collective-permute-start(f32[32,4,128]{2,1,0:T(4,128)S(1)} %get-tuple-element.38), channel_id=1, source_target_pairs={{0,4},{4,8},{8,12},{12,16},{16,20},{20,24},{24,28},{1,5},{5,9},{9,... | collective-permute-start | bytes 196616 | tf_op jit(solution)/shard_map/ppermute | solution.py:18
  26.5 1.2 bitcast_multiply_fusion.1
  27.7 13.0 %collective-permute-start.8 = (f32[32,4,128]{2,1,0:T(4,128)S(1)}, f32[32,4,128]{2,1,0:T(4,128)S(1)}, u32[]{:S(2)}, u32[]{:S(2)}) collective-permute-start(f32[32,4,128]{2,1,0:T(4,128)S(1)} %get-tuple-element.35), channel_id=1, source_target_pairs={{0,4},{4,8},{8,12},{12,16},{16,20},{20,24},{24,28},{1,5},{5,9},{9,... | collective-permute-start | bytes 196616 | tf_op jit(solution)/shard_map/ppermute | solution.py:18
  40.7 1.3 collective-permute-start.9
  44.6 1.3 collective-permute-start.3
  45.9 4.0 %collective-permute-start.2 = (f32[32,32,4]{2,1,0:T(8,128)S(1)}, f32[32,32,4]{2,1,0:T(8,128)S(1)}, u32[]{:S(2)}, u32[]{:S(2)}) collective-permute-start(f32[32,32,4]{2,1,0:T(8,128)S(1)} %get-tuple-element.31), channel_id=1, source_target_pairs={{0,1},{1,2},{2,3},{4,5},{5,6},{6,7},{8,9},{9,10},{10,11},{12,13},{... | collective-permute-start | bytes 49160 | tf_op jit(solution)/shard_map/ppermute | solution.py:18
  50.0 4.4 %collective-permute-done.9 = f32[32,4,128]{2,1,0:T(4,128)S(1)} collective-permute-done((f32[32,4,128]{2,1,0:T(4,128)S(1)}, f32[32,4,128]{2,1,0:T(4,128)S(1)}, u32[]{:S(2)}, u32[]{:S(2)}) %collective-permute-start.9) | collective-permute-done | bytes 65568 | tf_op jit(solution)/shard_map/ppermute | solution.py:20
  54.5 1.1 fusion.121
  55.6 1.3 collective-permute-start.11
  56.9 4.0 %collective-permute-start.10 = (f32[32,32,4]{2,1,0:T(8,128)}, f32[32,32,4]{2,1,0:T(8,128)S(1)}, u32[]{:S(2)}, u32[]{:S(2)}) collective-permute-start(f32[32,32,4]{2,1,0:T(8,128)} %get-tuple-element.23), channel_id=1, source_target_pairs={{0,1},{1,2},{2,3},{4,5},{5,6},{6,7},{8,9},{9,10},{10,11},{12,13},{... | collective-permute-start | bytes 49160 | tf_op jit(solution)/shard_map/ppermute | solution.py:18
  61.6 0.6 select_maximum_fusion.12
  62.7 2.4 fusion.110
  65.0 0.9 scatter_fusion
  66.0 0.7 fusion.126
  66.7 1.3 collective-permute-start.5
  68.0 13.3 %collective-permute-start.4 = (f32[32,4,128]{2,1,0:T(4,128)}, f32[32,4,128]{2,1,0:T(4,128)}, u32[]{:S(2)}, u32[]{:S(2)}) collective-permute-start(f32[32,4,128]{2,1,0:T(4,128)} %get-tuple-element.36), channel_id=1, source_target_pairs={{0,4},{4,8},{8,12},{12,16},{16,20},{20,24},{24,28},{1,5},{5,9},{9,... | collective-permute-start | bytes 196616 | tf_op jit(solution)/shard_map/ppermute | solution.py:18
  81.3 2.9 gather_fusion.1
  85.9 1.6 fusion.34
  87.6 1.0 pad_maximum_fusion.5
  88.8 1.3 collective-permute-start.7
  90.1 4.2 %collective-permute-start.6 = (f32[32,32,4]{2,1,0:T(8,128)S(1)}, f32[32,32,4]{2,1,0:T(8,128)S(1)}, u32[]{:S(2)}, u32[]{:S(2)}) collective-permute-start(f32[32,32,4]{2,1,0:T(8,128)S(1)} %get-tuple-element.27), channel_id=1, source_target_pairs={{0,1},{1,2},{2,3},{4,5},{5,6},{6,7},{8,9},{9,10},{10,11},{12,13},{... | collective-permute-start | bytes 49160 | tf_op jit(solution)/shard_map/ppermute | solution.py:18
  94.3 0.9 constant_dynamic-update-slice_fusion
  95.2 3.9 %collective-permute-done.7 = f32[32,32,4]{2,1,0:T(8,128)S(1)} collective-permute-done((f32[32,32,4]{2,1,0:T(8,128)S(1)}, f32[32,32,4]{2,1,0:T(8,128)S(1)}, u32[]{:S(2)}, u32[]{:S(2)}) %collective-permute-start.7) | collective-permute-done | bytes 16416 | tf_op jit(solution)/shard_map/ppermute | solution.py:20
  99.1 1.1 collective-permute-done.6
  100.2 1.5 pad_maximum_fusion.1
  101.7 1.5 select_maximum_fusion.8
  103.2 2.6 multiply_add_fusion
  105.9 0.9 scatter_fusion.1
  106.8 2.4 gather_fusion
  109.3 14.9 %scatter_fusion.2 = f32[32,24,128]{2,1,0:T(8,128)S(1)} fusion(f32[32,24,128]{2,1,0:T(8,128)S(1)} %fusion.34, s32[256]{0:T(256)S(1)} %bitcast.49, f32[256]{0:T(256)S(1)} %get-tuple-element.43), kind=kCustom, calls=%fused_computation.4 | custom fusion | flops 256 | bytes 6144 | tf_op jit(solution)/shard_map/scatter-add | solution.py:84
  124.2 0.9 fusion.109
  125.2 11.8 %collective-permute-start.12 = (f32[32,4,128]{2,1,0:T(4,128)S(1)}, f32[32,4,128]{2,1,0:T(4,128)S(1)}, u32[]{:S(2)}, u32[]{:S(2)}) collective-permute-start(f32[32,4,128]{2,1,0:T(4,128)S(1)} %get-tuple-element.33), channel_id=1, source_target_pairs={{0,4},{4,8},{8,12},{12,16},{16,20},{20,24},{24,28},{1,5},{5,9},{9,... | collective-permute-start | bytes 196616 | tf_op jit(solution)/shard_map/ppermute | solution.py:18
  136.9 1.3 collective-permute-start.13
  138.3 12.5 %collective-permute-done.13 = f32[32,4,128]{2,1,0:T(4,128)S(1)} collective-permute-done((f32[32,4,128]{2,1,0:T(4,128)S(1)}, f32[32,4,128]{2,1,0:T(4,128)S(1)}, u32[]{:S(2)}, u32[]{:S(2)}) %collective-permute-start.13) | collective-permute-done | bytes 65568 | tf_op jit(solution)/shard_map/ppermute | solution.py:20
  150.9 1.1 fusion.120
  152.0 1.3 collective-permute-start.15
  153.3 4.8 %collective-permute-start.14 = (f32[32,32,4]{2,1,0:T(8,128)}, f32[32,32,4]{2,1,0:T(8,128)S(1)}, u32[]{:S(2)}, u32[]{:S(2)}) collective-permute-start(f32[32,32,4]{2,1,0:T(8,128)} %get-tuple-element.19), channel_id=1, source_target_pairs={{0,1},{1,2},{2,3},{4,5},{5,6},{6,7},{8,9},{9,10},{10,11},{12,13},{... | collective-permute-start | bytes 49160 | tf_op jit(solution)/shard_map/ppermute | solution.py:18
  158.7 4.1 %collective-permute-done.15 = f32[32,32,4]{2,1,0:T(8,128)S(1)} collective-permute-done((f32[32,32,4]{2,1,0:T(8,128)}, f32[32,32,4]{2,1,0:T(8,128)S(1)}, u32[]{:S(2)}, u32[]{:S(2)}) %collective-permute-start.15) | collective-permute-done | bytes 16416 | tf_op jit(solution)/shard_map/ppermute | solution.py:20
  162.9 1.6 collective-permute-done.14
  165.0 0.6 select_maximum_fusion
  165.7 1.6 fusion.8
  167.3 14.9 %scatter_fusion.3 = f32[32,24,128]{2,1,0:T(8,128)S(1)} fusion(f32[32,24,128]{2,1,0:T(8,128)S(1)} %fusion.8, s32[256]{0:T(256)S(1)} %bitcast.50, f32[256]{0:T(256)S(1)} %get-tuple-element.42), kind=kCustom, calls=%fused_computation.5 | custom fusion | flops 256 | bytes 6144 | tf_op jit(solution)/shard_map/scatter-add | solution.py:84
  182.2 83.5 %reduce-scatter.2.cloned.1.call-done = f32[2,24,128]{2,1,0:T(8,128)} async-done(((f32[32,24,128]{2,1,0:T(8,128)}), f32[2,24,128]{2,1,0:T(8,128)}) %reduce-scatter.2.cloned.1.call-update) | async-done | bytes 24592 | tf_op jit(solution)/shard_map/reduce_scatter | solution.py:96
  265.7 0.7 multiply_subtract_fusion
  266.5 35.6 %all_gather.3 = f32[32,24,128]{2,1,0:T(8,128)S(1)} all-gather(f32[2,24,128]{2,1,0:T(8,128)S(1)} %multiply_subtract_fusion), channel_id=1, replica_groups=mesh['shot'=16,'px'=8,'py'=4] {'shot'}, dimensions={0}, use_global_device_ids=true | all-gather | bytes 417792 | tf_op jit(solution)/shard_map/all_gather | solution.py:100
  302.0 0.7 copy.29
  (71 shorter events, 6.4 us)
Async XLA Ops:
  7.2 37.2 %copy-start.1 = (f32[1,32,24,128]{3,2,1,0:T(8,128)S(1)}, f32[1,32,24,128]{3,2,1,0:T(8,128)}, u32[]{:S(2)}) copy-start(f32[1,32,24,128]{3,2,1,0:T(8,128)} %param.11) | copy-start | bytes 1179652
  7.2 34.8 %copy-start.16 = (s32[1,8,3]{1,0,2:T(1,128)S(1)}, s32[1,8,3]{1,0,2:T(1,128)}, u32[]{:S(2)}) copy-start(s32[1,8,3]{1,0,2:T(1,128)} %param.15) | copy-start | bytes 292
  7.2 34.9 %copy-start.18 = (f32[1,2,8]{2,1,0:T(2,128)S(1)}, f32[1,2,8]{2,1,0:T(2,128)}, u32[]{:S(2)}) copy-start(f32[1,2,8]{2,1,0:T(2,128)} %param.16) | copy-start | bytes 196
  7.2 35.9 %copy-start.12 = (s32[1,256,3]{1,0,2:T(1,128)S(1)}, s32[1,256,3]{1,0,2:T(1,128)}, u32[]{:S(2)}) copy-start(s32[1,256,3]{1,0,2:T(1,128)} %param.17) | copy-start | bytes 9220
  7.2 35.9 %copy-start.14 = (f32[1,2,256]{2,1,0:T(2,128)S(1)}, f32[1,2,256]{2,1,0:T(2,128)}, u32[]{:S(2)}) copy-start(f32[1,2,256]{2,1,0:T(2,128)} %param.18) | copy-start | bytes 6148
  7.2 258.5 %reduce-scatter.2.cloned.1.call-start = ((), (), s32[]{:S(2)}) async-start(), calls=%async_computation.1 | async-start | bytes 417792 | tf_op jit(solution)/shard_map/reduce_scatter | solution.py:96
  8.3 36.0 %collective-permute-start.1 = (f32[32,4,128]{2,1,0:T(4,128)S(1)}, f32[32,4,128]{2,1,0:T(4,128)S(1)}, u32[]{:S(2)}, u32[]{:S(2)}) collective-permute-start(f32[32,4,128]{2,1,0:T(4,128)S(1)} %get-tuple-element.39), channel_id=1, source_target_pairs={{4,0},{8,4},{12,8},{16,12},{20,16},{24,20},{28,24},{5,1},{9,5},{13... | collective-permute-start | bytes 196616 | tf_op jit(solution)/shard_map/ppermute | solution.py:20
  9.6 34.7 %collective-permute-start = (f32[32,4,128]{2,1,0:T(4,128)S(1)}, f32[32,4,128]{2,1,0:T(4,128)S(1)}, u32[]{:S(2)}, u32[]{:S(2)}) collective-permute-start(f32[32,4,128]{2,1,0:T(4,128)S(1)} %get-tuple-element.38), channel_id=1, source_target_pairs={{0,4},{4,8},{8,12},{12,16},{16,20},{20,24},{24,28},{1,5},{5,9},{9,... | collective-permute-start | bytes 196616 | tf_op jit(solution)/shard_map/ppermute | solution.py:18
  27.7 22.3 %collective-permute-start.8 = (f32[32,4,128]{2,1,0:T(4,128)S(1)}, f32[32,4,128]{2,1,0:T(4,128)S(1)}, u32[]{:S(2)}, u32[]{:S(2)}) collective-permute-start(f32[32,4,128]{2,1,0:T(4,128)S(1)} %get-tuple-element.35), channel_id=1, source_target_pairs={{0,4},{4,8},{8,12},{12,16},{16,20},{20,24},{24,28},{1,5},{5,9},{9,... | collective-permute-start | bytes 196616 | tf_op jit(solution)/shard_map/ppermute | solution.py:18
  40.7 13.7 %collective-permute-start.9 = (f32[32,4,128]{2,1,0:T(4,128)S(1)}, f32[32,4,128]{2,1,0:T(4,128)S(1)}, u32[]{:S(2)}, u32[]{:S(2)}) collective-permute-start(f32[32,4,128]{2,1,0:T(4,128)S(1)} %get-tuple-element.34), channel_id=1, source_target_pairs={{4,0},{8,4},{12,8},{16,12},{20,16},{24,20},{28,24},{5,1},{9,5},{13... | collective-permute-start | bytes 196616 | tf_op jit(solution)/shard_map/ppermute | solution.py:20
  44.6 16.3 %collective-permute-start.3 = (f32[32,32,4]{2,1,0:T(8,128)S(1)}, f32[32,32,4]{2,1,0:T(8,128)S(1)}, u32[]{:S(2)}, u32[]{:S(2)}) collective-permute-start(f32[32,32,4]{2,1,0:T(8,128)S(1)} %get-tuple-element.30), channel_id=1, source_target_pairs={{1,0},{2,1},{3,2},{5,4},{6,5},{7,6},{9,8},{10,9},{11,10},{13,12},{... | collective-permute-start | bytes 49160 | tf_op jit(solution)/shard_map/ppermute | solution.py:20
  45.9 15.0 %collective-permute-start.2 = (f32[32,32,4]{2,1,0:T(8,128)S(1)}, f32[32,32,4]{2,1,0:T(8,128)S(1)}, u32[]{:S(2)}, u32[]{:S(2)}) collective-permute-start(f32[32,32,4]{2,1,0:T(8,128)S(1)} %get-tuple-element.31), channel_id=1, source_target_pairs={{0,1},{1,2},{2,3},{4,5},{5,6},{6,7},{8,9},{9,10},{10,11},{12,13},{... | collective-permute-start | bytes 49160 | tf_op jit(solution)/shard_map/ppermute | solution.py:18
  55.6 28.6 %collective-permute-start.11 = (f32[32,32,4]{2,1,0:T(8,128)}, f32[32,32,4]{2,1,0:T(8,128)S(1)}, u32[]{:S(2)}, u32[]{:S(2)}) collective-permute-start(f32[32,32,4]{2,1,0:T(8,128)} %get-tuple-element.22), channel_id=1, source_target_pairs={{1,0},{2,1},{3,2},{5,4},{6,5},{7,6},{9,8},{10,9},{11,10},{13,12},{... | collective-permute-start | bytes 49160 | tf_op jit(solution)/shard_map/ppermute | solution.py:20
  56.9 27.3 %collective-permute-start.10 = (f32[32,32,4]{2,1,0:T(8,128)}, f32[32,32,4]{2,1,0:T(8,128)S(1)}, u32[]{:S(2)}, u32[]{:S(2)}) collective-permute-start(f32[32,32,4]{2,1,0:T(8,128)} %get-tuple-element.23), channel_id=1, source_target_pairs={{0,1},{1,2},{2,3},{4,5},{5,6},{6,7},{8,9},{9,10},{10,11},{12,13},{... | collective-permute-start | bytes 49160 | tf_op jit(solution)/shard_map/ppermute | solution.py:18
  61.5 1.0 copy-start.4
  61.5 1.1 copy-start.8
  62.6 2.4 copy-start.17
  66.0 37.3 %copy-start = (f32[32,24,128]{2,1,0:T(8,128)}, f32[32,24,128]{2,1,0:T(8,128)S(1)}, u32[]{:S(2)}) copy-start(f32[32,24,128]{2,1,0:T(8,128)S(1)} %scatter_fusion) | copy-start | bytes 1179652
  66.7 20.9 %collective-permute-start.5 = (f32[32,4,128]{2,1,0:T(4,128)}, f32[32,4,128]{2,1,0:T(4,128)}, u32[]{:S(2)}, u32[]{:S(2)}) collective-permute-start(f32[32,4,128]{2,1,0:T(4,128)} %get-tuple-element.37), channel_id=1, source_target_pairs={{4,0},{8,4},{12,8},{16,12},{20,16},{24,20},{28,24},{5,1},{9,5},{13... | collective-permute-start | bytes 196616 | tf_op jit(solution)/shard_map/ppermute | solution.py:20
  68.0 19.6 %collective-permute-start.4 = (f32[32,4,128]{2,1,0:T(4,128)}, f32[32,4,128]{2,1,0:T(4,128)}, u32[]{:S(2)}, u32[]{:S(2)}) collective-permute-start(f32[32,4,128]{2,1,0:T(4,128)} %get-tuple-element.36), channel_id=1, source_target_pairs={{0,4},{4,8},{8,12},{12,16},{16,20},{20,24},{24,28},{1,5},{5,9},{9,... | collective-permute-start | bytes 196616 | tf_op jit(solution)/shard_map/ppermute | solution.py:18
  84.8 1.0 copy-start.5
  84.8 1.1 copy-start.9
  88.8 10.3 %collective-permute-start.7 = (f32[32,32,4]{2,1,0:T(8,128)S(1)}, f32[32,32,4]{2,1,0:T(8,128)S(1)}, u32[]{:S(2)}, u32[]{:S(2)}) collective-permute-start(f32[32,32,4]{2,1,0:T(8,128)S(1)} %get-tuple-element.26), channel_id=1, source_target_pairs={{1,0},{2,1},{3,2},{5,4},{6,5},{7,6},{9,8},{10,9},{11,10},{13,12},{... | collective-permute-start | bytes 49160 | tf_op jit(solution)/shard_map/ppermute | solution.py:20
  90.1 10.1 %collective-permute-start.6 = (f32[32,32,4]{2,1,0:T(8,128)S(1)}, f32[32,32,4]{2,1,0:T(8,128)S(1)}, u32[]{:S(2)}, u32[]{:S(2)}) collective-permute-start(f32[32,32,4]{2,1,0:T(8,128)S(1)} %get-tuple-element.27), channel_id=1, source_target_pairs={{0,1},{1,2},{2,3},{4,5},{5,6},{6,7},{8,9},{9,10},{10,11},{12,13},{... | collective-permute-start | bytes 49160 | tf_op jit(solution)/shard_map/ppermute | solution.py:18
  103.2 2.7 copy-start.13
  105.9 3.4 %copy-start.10 = (f32[1,1,256]{2,1,0:T(1,128)S(1)}, f32[1,1,256]{2,1,0:T(1,128)}, u32[]{:S(2)}) copy-start(f32[1,1,256]{2,1,0:T(1,128)} %get-tuple-element.41) | copy-start | bytes 3076
  105.9 3.4 %copy-start.11 = (f32[256]{0:T(256)S(1)}, f32[256]{0:T(256)}, u32[]{:S(2)}) copy-start(f32[256]{0:T(256)} %gather_fusion.1) | copy-start | bytes 3076
  105.9 3.4 %copy-start.15 = (pred[256]{0:T(512)(128)(4,1)S(1)}, pred[256]{0:T(512)(128)(4,1)}, u32[]{:S(2)}) copy-start(pred[256]{0:T(512)(128)(4,1)} %and_reduce_fusion) | copy-start | bytes 772
  106.8 17.4 %copy-start.3 = (f32[32,24,128]{2,1,0:T(8,128)}, f32[32,24,128]{2,1,0:T(8,128)S(1)}, u32[]{:S(2)}) copy-start(f32[32,24,128]{2,1,0:T(8,128)S(1)} %scatter_fusion.1) | copy-start | bytes 1179652
  109.2 15.0 %copy-start.7 = (f32[32,24,128]{2,1,0:T(8,128)S(1)}, f32[32,24,128]{2,1,0:T(8,128)}, u32[]{:S(2)}) copy-start(f32[32,24,128]{2,1,0:T(8,128)} %get-tuple-element.13) | copy-start | bytes 1179652
  124.2 41.4 %copy-start.2 = (f32[32,24,128]{2,1,0:T(8,128)}, f32[32,24,128]{2,1,0:T(8,128)S(1)}, u32[]{:S(2)}) copy-start(f32[32,24,128]{2,1,0:T(8,128)S(1)} %scatter_fusion.2) | copy-start | bytes 1179652
  125.2 13.1 %collective-permute-start.12 = (f32[32,4,128]{2,1,0:T(4,128)S(1)}, f32[32,4,128]{2,1,0:T(4,128)S(1)}, u32[]{:S(2)}, u32[]{:S(2)}) collective-permute-start(f32[32,4,128]{2,1,0:T(4,128)S(1)} %get-tuple-element.33), channel_id=1, source_target_pairs={{0,4},{4,8},{8,12},{12,16},{16,20},{20,24},{24,28},{1,5},{5,9},{9,... | collective-permute-start | bytes 196616 | tf_op jit(solution)/shard_map/ppermute | solution.py:18
  136.9 13.8 %collective-permute-start.13 = (f32[32,4,128]{2,1,0:T(4,128)S(1)}, f32[32,4,128]{2,1,0:T(4,128)S(1)}, u32[]{:S(2)}, u32[]{:S(2)}) collective-permute-start(f32[32,4,128]{2,1,0:T(4,128)S(1)} %get-tuple-element.32), channel_id=1, source_target_pairs={{4,0},{8,4},{12,8},{16,12},{20,16},{24,20},{28,24},{5,1},{9,5},{13... | collective-permute-start | bytes 196616 | tf_op jit(solution)/shard_map/ppermute | solution.py:20
  152.0 10.9 %collective-permute-start.15 = (f32[32,32,4]{2,1,0:T(8,128)}, f32[32,32,4]{2,1,0:T(8,128)S(1)}, u32[]{:S(2)}, u32[]{:S(2)}) collective-permute-start(f32[32,32,4]{2,1,0:T(8,128)} %get-tuple-element.18), channel_id=1, source_target_pairs={{1,0},{2,1},{3,2},{5,4},{6,5},{7,6},{9,8},{10,9},{11,10},{13,12},{... | collective-permute-start | bytes 49160 | tf_op jit(solution)/shard_map/ppermute | solution.py:20
  153.3 11.2 %collective-permute-start.14 = (f32[32,32,4]{2,1,0:T(8,128)}, f32[32,32,4]{2,1,0:T(8,128)S(1)}, u32[]{:S(2)}, u32[]{:S(2)}) collective-permute-start(f32[32,32,4]{2,1,0:T(8,128)} %get-tuple-element.19), channel_id=1, source_target_pairs={{0,1},{1,2},{2,3},{4,5},{5,6},{6,7},{8,9},{9,10},{10,11},{12,13},{... | collective-permute-start | bytes 49160 | tf_op jit(solution)/shard_map/ppermute | solution.py:18
  182.2 120.6 %copy-start.6 = (f32[32,24,128]{2,1,0:T(8,128)}, f32[32,24,128]{2,1,0:T(8,128)S(1)}, u32[]{:S(2)}) copy-start(f32[32,24,128]{2,1,0:T(8,128)S(1)} %scatter_fusion.3) | copy-start | bytes 1179652
Sparse Core Ops, SparseCore 0:
  158.9 106.8 reduce-scatter.1
where the time goes:
time: 311 us; the launch traced here: 310 us
  waiting for transfers between devices  111 us (36%)
  starting transfers between devices  82.3 us (26%)
  other arithmetic  52.1 us (17%)
  blocking collectives  35.6 us (11%)
  between operations  15.3 us (5%)
  local copies, waits for them, and re-layouts  13.1 us (4%)
    reduce_scatter x1, waiting for transfers between devices, local(): summed = lax.psum_scatter(term, 'shot', scatter_dimension=0, tiled=True)  83.5 us
    ppermute x8, starting transfers between devices, extended_2(): lax.ppermute(tail, axis, [(i, (i + 1) % count) for i in range(ends)])  72 us
    all_gather x1, blocking collectives, local(): new_speed = lax.all_gather(new_slab, 'shot', axis=0, tiled=True)  35.6 us
    scatter-add x2, other arithmetic, add_receivers(): field.at[rec_depth, rec_first, rec_second]  29.8 us
    ppermute x8, waiting for transfers between devices, extended_2(): lax.ppermute(head, axis, [((i + 1) % count, i) for i in range(ends)])  25 us
    ppermute x8, starting transfers between devices, extended_2(): lax.ppermute(head, axis, [((i + 1) % count, i) for i in range(ends)])  10.3 us
    concatenate x12, other arithmetic, extended_2(): jnp.concatenate([lax.ppermute(tail, axis, [(i, (i + 1) % count) for i in...  7.68 us
  transfers between devices with their start and end apart: 17, of which 7 were waited for; matrix products, arithmetic and copies ran while one was open for 11% of the time, Pallas kernels for 0%

commit v1 on v0

v1 whole, which is shorter than its diff:
```python
import functools

import jax
import jax.numpy as jnp
from jax import lax
from jax.experimental import pallas as pl
from jax.experimental.pallas import tpu as pltpu
from jax.sharding import PartitionSpec as P

WEIGHTS = (-205.0 / 72.0, 1.6, -0.2, 8.0 / 315.0, -1.0 / 560.0)
TIME_FACTOR = 0.009
MESH = pl.DeviceIdType.MESH
NZ, ROWS, COLS = 32, 24, 128
NREC, NSRC = 256, 8
TILES = ROWS // 8
UNROLL = 4

(F_L, F_R, F_PL, F_PR, C_L, C_R, C_PL, C_PR, M_L, M_R, M_PL, M_PR, D_L, D_R, D_PL, D_PR) = range(16)
SUM_A, SUM_B, SUM_C, SUM_D, ALL_D, ALL_C, ALL_B, ALL_A = range(16, 24)
N_SEMS = 24


def kernel(
    before_h, now_h, after_h, adj_h, speed_h, src_pos, src_amp, rec_pos, observed, rate,
    mid_o, last_o, adj_mid_o, adj_last_o, new_o, grad_o,
    fnow, fmid, cadj, cmid,
    before, after, adj, speed, lap1, last, amid, alast,
    s_one, s_two, count, obs_two, obs_three,
    pack, halo,
    term, ra, sa, rb, sb, rc, sc, rd, grad, new,
    in_sem, out_sem, send_sem, recv_sem,
):
    shot, px, py = lax.axis_index("shot"), lax.axis_index("px"), lax.axis_index("py")
    n_px, n_py = lax.axis_size("px"), lax.axis_size("py")
    core, z_lo = lax.rem(shot, 2), shot // 2
    bit0, bit1, bit2 = lax.rem(z_lo, 2), lax.rem(z_lo // 2, 2), z_lo // 4
    has_left, has_right = px > 0, px < n_px - 1
    has_prev, has_next = py > 0, py < n_py - 1
    left = (shot, lax.rem(px + n_px - 1, n_px), py)
    right = (shot, lax.rem(px + 1, n_px), py)
    prev = (shot, px, lax.rem(py + n_py - 1, n_py))
    after_py = (shot, px, lax.rem(py + 1, n_py))
    mate = (shot + 1 - 2 * core, px, py)
    near1 = (shot + 2 * (1 - 2 * bit0), px, py)
    near2 = (shot + 4 * (1 - 2 * bit1), px, py)
    near4 = (shot + 8 * (1 - 2 * bit2), px, py)

    inner = (slice(4, 4 + NZ), slice(8, 8 + ROWS), slice(None))
    load_now = pltpu.make_async_copy(now_h, fnow.at[inner], in_sem.at[0])
    load_adj = pltpu.make_async_copy(adj_h, adj, in_sem.at[1])
    load_speed = pltpu.make_async_copy(speed_h, speed, in_sem.at[2])
    load_before = pltpu.make_async_copy(before_h, before, in_sem.at[3])
    load_after = pltpu.make_async_copy(after_h, after, in_sem.at[4])
    for load in (load_now, load_adj, load_speed, load_before, load_after):
        load.start()

    barrier = pltpu.get_barrier_semaphore()
    partners = (left, right, prev, after_py, mate, near1, near2, near4)
    for device in partners:
        pl.semaphore_signal(barrier, inc=1, device_id=device, device_id_type=MESH)

    for field in (fnow, fmid, cadj, cmid):
        for plane in (0, 1, 2, 3, NZ + 4, NZ + 5, NZ + 6, NZ + 7):
            field[plane] = jnp.zeros((ROWS + 16, COLS), jnp.float32)

    @pl.when(px == 0)
    def _():
        def body(z, _):
            for field in (fnow, fmid, cadj, cmid):
                field[z + 4, 0:8, :] = jnp.zeros((8, COLS), jnp.float32)
            return 0
        lax.fori_loop(0, NZ, body, 0)

    @pl.when(px == n_px - 1)
    def _():
        def body(z, _):
            for field in (fnow, fmid, cadj, cmid):
                field[z + 4, 8 + ROWS:16 + ROWS, :] = jnp.zeros((8, COLS), jnp.float32)
            return 0
        lax.fori_loop(0, NZ, body, 0)

    @pl.when(py == 0)
    def _():
        for k in range(4):
            halo[2 * k] = jnp.zeros((ROWS, COLS), jnp.float32)

    @pl.when(py == n_py - 1)
    def _():
        for k in range(4):
            halo[2 * k + 1] = jnp.zeros((ROWS, COLS), jnp.float32)

    lane = lax.broadcasted_iota(jnp.int32, (8, COLS), 1)
    group = lane // 4

    def remote(src, dst, sem, device):
        return pltpu.make_async_remote_copy(
            src_ref=src, dst_ref=dst, send_sem=send_sem.at[sem], recv_sem=recv_sem.at[sem],
            device_id=device, device_id_type=MESH,
        )

    class Halo:
        def __init__(self, k, field):
            low, high = slice(8, 12), slice(4 + ROWS, 8 + ROWS)
            over, under = slice(8 + ROWS, 12 + ROWS), slice(4, 8)
            depth = slice(4, 4 + NZ)
            self.to_left = remote(field.at[depth, low, :], field.at[depth, over, :], 4 * k, left)
            self.to_right = remote(field.at[depth, high, :], field.at[depth, under, :], 4 * k + 1, right)
            self.to_prev = remote(pack.at[2 * k], halo.at[2 * k + 1], 4 * k + 2, prev)
            self.to_next = remote(pack.at[2 * k + 1], halo.at[2 * k], 4 * k + 3, after_py)

        def send_left(self):
            pl.when(has_left)(self.to_left.start)

        def send_right(self):
            pl.when(has_right)(self.to_right.start)

        def send_lanes(self):
            pl.when(has_prev)(self.to_prev.start)
            pl.when(has_next)(self.to_next.start)

        def wait_left(self):
            pl.when(has_left)(self.to_right.wait_recv)

        def wait_right(self):
            pl.when(has_right)(self.to_left.wait_recv)

        def wait_lanes(self):
            pl.when(has_next)(self.to_prev.wait_recv)
            pl.when(has_prev)(self.to_next.wait_recv)

        def finish(self):
            pl.when(has_left)(self.to_left.wait_send)
            pl.when(has_right)(self.to_right.wait_send)
            pl.when(has_prev)(self.to_prev.wait_send)
            pl.when(has_next)(self.to_next.wait_send)

    halo_now, halo_cadj, halo_mid, halo_cmid = (
        Halo(k, field) for k, field in enumerate((fnow, cadj, fmid, cmid))
    )

    def packed(z, value, carry):
        to_prev, to_next = carry
        moved = pltpu.roll(value, lax.rem(4 * z + 4, COLS), 1)
        return (
            jnp.where(group == lax.rem(z + 1, NZ), moved, to_prev),
            jnp.where(group == z, moved, to_next),
        )

    def laplace(field, k, z, tile):
        row = 8 + 8 * tile
        centre = field[z + 4, row:row + 8, :]
        from_prev = pltpu.roll(halo[2 * k, 8 * tile:8 * tile + 8, :], COLS - 4 - 4 * z, 1)
        from_next = pltpu.roll(halo[2 * k + 1, 8 * tile:8 * tile + 8, :], COLS - 4 - 4 * z, 1)
        total = (3.0 * WEIGHTS[0]) * centre
        for r in range(1, 5):
            near = field[z + 4 + r, row:row + 8, :] + field[z + 4 - r, row:row + 8, :]
            near = near + field[z + 4, row + r:row + r + 8, :] + field[z + 4, row - r:row - r + 8, :]
            near = near + pltpu.roll(jnp.where(lane >= COLS - r, from_prev, centre), r, 1)
            near = near + pltpu.roll(jnp.where(lane < r, from_next, centre), COLS - r, 1)
            total = total + WEIGHTS[r] * near
        return centre, total

    zero = jnp.zeros((8, COLS), jnp.float32)

    def over_depth(tile, k, step):
        def body(z, carry):
            value = step(z)
            return packed(z, value, carry) if k is not None else carry
        carry = lax.fori_loop(0, NZ, body, (zero, zero) if k is not None else 0, unroll=UNROLL)
        if k is not None:
            pack[2 * k, 8 * tile:8 * tile + 8, :] = carry[0]
            pack[2 * k + 1, 8 * tile:8 * tile + 8, :] = carry[1]

    load_now.wait()
    pl.semaphore_wait(barrier, len(partners))
    halo_now.send_left()
    halo_now.send_right()
    for tile in range(TILES):
        over_depth(tile, 0, lambda z: fnow[z + 4, 8 + 8 * tile:16 + 8 * tile, :])
    halo_now.send_lanes()

    load_adj.wait()
    load_speed.wait()

    def coef_at(z, rows):
        value = speed[z, rows, :]
        return TIME_FACTOR * value * value

    for tile in range(TILES):
        rows, ext = slice(8 * tile, 8 * tile + 8), slice(8 + 8 * tile, 16 + 8 * tile)

        def scale(z):
            value = coef_at(z, rows) * adj[z, rows, :]
            cadj[z + 4, ext, :] = value
            return value

        over_depth(tile, 1, scale)
    halo_cadj.send_left()
    halo_cadj.send_right()
    halo_cadj.send_lanes()

    first_start, second_start = px * ROWS, py * COLS
    place = lax.broadcasted_iota(jnp.int32, (8, COLS), 0) * COLS + lane
    keys, amps = [], []
    for j in range(NSRC):
        first, second = src_pos[j, 1] - first_start, src_pos[j, 2] - second_start
        owned = (first >= 0) & (first < ROWS) & (second >= 0) & (second < COLS)
        keys.append(jnp.where(owned, (src_pos[j, 0] * ROWS + first) * COLS + second, -1))
        amps.append((src_amp[0, j], src_amp[1, j]))
    for tile in range(TILES):
        rows = slice(8 * tile, 8 * tile + 8)

        def sources(z, _):
            here = place + (z * ROWS + 8 * tile) * COLS
            one, two = zero, zero
            for key, (amp_one, amp_two) in zip(keys, amps):
                hit = here == key
                one = one + jnp.where(hit, amp_one, 0.0)
                two = two + jnp.where(hit, amp_two, 0.0)
            s_one[z, rows, :] = one
            s_two[z, rows, :] = two
            return 0

        lax.fori_loop(0, NZ, sources, 0)

    first = rec_pos[:, 1:2] - first_start
    second = rec_pos[:, 2:3] - second_start
    inside = (first >= 0) & (first < ROWS)
    cell = jnp.where(inside, rec_pos[:, 0:1] * ROWS + first, -1).astype(jnp.float32)
    cell_row = jnp.transpose(jnp.broadcast_to(cell, (NREC, COLS)))[0:1, :]
    data = jnp.transpose(observed[...])
    column = lax.broadcasted_iota(jnp.int32, (NREC, COLS), 1) == second
    parts = [column.astype(jnp.float32).astype(jnp.bfloat16)]
    for k in range(2):
        rest = jnp.where(column, jnp.broadcast_to(data[:, k:k + 1], (NREC, COLS)), 0.0)
        for _ in range(3):
            part = rest.astype(jnp.bfloat16)
            rest = rest - part.astype(jnp.float32)
            parts.append(part)
    DEPTHS = 8

    def receivers(step, _):
        base = step * (DEPTHS * ROWS)
        index = lax.broadcasted_iota(jnp.int32, (DEPTHS * ROWS, NREC), 0) + base
        hot = (index.astype(jnp.float32) == cell_row).astype(jnp.float32).astype(jnp.bfloat16)
        sums = [jnp.dot(hot, part, preferred_element_type=jnp.float32) for part in parts]
        depths = pl.ds(step * DEPTHS, DEPTHS)
        count[depths] = sums[0].reshape(DEPTHS, ROWS, COLS)
        obs_two[depths] = (sums[1] + sums[2] + sums[3]).reshape(DEPTHS, ROWS, COLS)
        obs_three[depths] = (sums[4] + sums[5] + sums[6]).reshape(DEPTHS, ROWS, COLS)
        return 0

    lax.fori_loop(0, NZ // DEPTHS, receivers, 0)

    load_before.wait()
    halo_now.wait_lanes()

    def mid_tile(tile):
        rows, ext = slice(8 * tile, 8 * tile + 8), slice(8 + 8 * tile, 16 + 8 * tile)

        def step(z):
            centre, lap = laplace(fnow, 0, z, tile)
            lap1[z, rows, :] = lap
            value = 2.0 * centre - before[z, rows, :] + coef_at(z, rows) * lap + s_one[z, rows, :]
            fmid[z + 4, ext, :] = value
            return value

        over_depth(tile, 2, step)

    mid_tile(1)
    halo_now.wait_left()
    mid_tile(0)
    halo_mid.send_left()
    halo_now.wait_right()
    mid_tile(2)
    halo_mid.send_right()
    halo_mid.send_lanes()
    store_mid = pltpu.make_async_copy(fmid.at[inner], mid_o, out_sem.at[0])
    store_mid.start()

    load_after.wait()
    halo_cadj.wait_lanes()

    def base_tile(tile):
        rows = slice(8 * tile, 8 * tile + 8)

        def step(z):
            _, lap = laplace(cadj, 1, z, tile)
            amid[z, rows, :] = 2.0 * adj[z, rows, :] - after[z, rows, :] + lap - obs_three[z, rows, :]

        over_depth(tile, None, step)

    base_tile(1)
    halo_cadj.wait_left()
    base_tile(0)
    halo_cadj.wait_right()
    base_tile(2)

    halo_mid.wait_lanes()

    def last_tile(tile):
        rows, ext = slice(8 * tile, 8 * tile + 8), slice(8 + 8 * tile, 16 + 8 * tile)

        def step(z):
            centre, lap = laplace(fmid, 2, z, tile)
            velocity = speed[z, rows, :]
            coef = TIME_FACTOR * velocity * velocity
            value = 2.0 * centre - fnow[z + 4, ext, :] + coef * lap + s_two[z, rows, :]
            last[z, rows, :] = value
            adjoint = amid[z, rows, :] + count[z, rows, :] * value
            amid[z, rows, :] = adjoint
            image = adjoint * lap1[z, rows, :] + adj[z, rows, :] * lap
            owner = z // 2
            term[owner // 8, lax.rem(owner // 4, 2), lax.rem(owner // 2, 2), lax.rem(owner, 2), lax.rem(z, 2), rows, :] = (
                2.0 * TIME_FACTOR * velocity * image
            )
            scaled = coef * adjoint
            cmid[z + 4, ext, :] = scaled
            return scaled

        over_depth(tile, 3, step)

    last_tile(1)
    halo_mid.wait_left()
    last_tile(0)
    halo_cmid.send_left()
    halo_mid.wait_right()
    last_tile(2)
    sum_a = remote(term.at[:, :, :, 1 - core], ra, SUM_A, mate)
    sum_a.start()
    halo_cmid.send_right()
    halo_cmid.send_lanes()
    store_last = pltpu.make_async_copy(last, last_o, out_sem.at[1])
    store_last.start()
    store_amid = pltpu.make_async_copy(amid, adj_mid_o, out_sem.at[2])
    store_amid.start()

    sum_a.wait_recv()

    def add_a(step, _):
        i, j = step // 2, lax.rem(step, 2)
        for k in range(2):
            sa[i, j, k] = term[i, j, k, core] + ra[i, j, k]
        return 0

    lax.fori_loop(0, 4, add_a, 0)
    sum_b = remote(sa.at[:, :, 1 - bit0], rb, SUM_B, near1)
    sum_b.start()
    sum_b.wait_recv()
    for i in range(2):
        for j in range(2):
            sb[i, j] = sa[i, j, bit0] + rb[i, j]
    sum_c = remote(sb.at[:, 1 - bit1], rc, SUM_C, near2)
    sum_c.start()

    def adj_tile(tile):
        rows = slice(8 * tile, 8 * tile + 8)
        ext = slice(8 + 8 * tile, 16 + 8 * tile)

        def step(z):
            _, lap = laplace(cmid, 3, z, tile)
            alast[z, rows, :] = (
                2.0 * amid[z, rows, :] - adj[z, rows, :] + lap
                + (count[z, rows, :] * fmid[z + 4, ext, :] - obs_two[z, rows, :])
            )

        over_depth(tile, None, step)

    halo_cmid.wait_lanes()
    adj_tile(1)

    sum_c.wait_recv()
    for i in range(2):
        sc[i] = sb[i, bit1] + rc[i]
    sum_d = remote(sc.at[1 - bit2], rd, SUM_D, near4)
    sum_d.start()
    sum_d.wait_recv()
    total = sc[bit2] + rd[...]
    grad[...] = total
    new[bit2, bit1, bit0, core] = speed[pl.ds(2 * shot, 2)] - rate[0] * total
    store_grad = pltpu.make_async_copy(grad, grad_o, out_sem.at[3])
    store_grad.start()

    own = new.at[bit2, bit1, bit0, core]
    all_d = remote(own, own, ALL_D, near4)
    all_d.start()
    all_d.wait_recv()
    own = new.at[:, bit1, bit0, core]
    all_c = remote(own, own, ALL_C, near2)
    all_c.start()
    all_c.wait_recv()
    own = new.at[:, :, bit0, core]
    all_b = remote(own, own, ALL_B, near1)
    all_b.start()
    all_b.wait_recv()
    own = new.at[:, :, :, core]
    all_a = remote(own, own, ALL_A, mate)
    all_a.start()

    halo_cmid.wait_left()
    adj_tile(0)
    halo_cmid.wait_right()
    adj_tile(2)
    store_alast = pltpu.make_async_copy(alast, adj_last_o, out_sem.at[4])
    store_alast.start()

    all_a.wait_recv()
    store_new = pltpu.make_async_copy(new, new_o, out_sem.at[5])
    store_new.start()

    for field in (halo_now, halo_cadj, halo_mid, halo_cmid):
        field.finish()
    for copy in (sum_a, sum_b, sum_c, sum_d, all_d, all_c, all_b, all_a):
        copy.wait_send()
    for store in (store_mid, store_last, store_amid, store_grad, store_alast, store_new):
        store.wait()


def local(before, now, after, adj, speed, src_pos, src_amp, rec_pos, observed, rate):
    f32 = jnp.float32
    block = (NZ, ROWS, COLS)
    padded = (NZ + 8, ROWS + 16, COLS)
    slab = (2, ROWS, COLS)

    def vmem(*shape):
        return pltpu.VMEM(shape, f32)

    anywhere = pl.BlockSpec(memory_space=pl.ANY)
    in_vmem = pl.BlockSpec(memory_space=pltpu.VMEM)
    in_smem = pl.BlockSpec(memory_space=pltpu.SMEM)
    outs = pl.pallas_call(
        kernel,
        out_shape=[jax.ShapeDtypeStruct(block, f32)] * 4
        + [jax.ShapeDtypeStruct((2, 2, 2, 2) + slab, f32), jax.ShapeDtypeStruct(slab, f32)],
        in_specs=[anywhere] * 5 + [in_smem, in_smem, in_vmem, in_vmem, in_smem],
        out_specs=[anywhere] * 6,
        scratch_shapes=[vmem(*padded)] * 4
        + [vmem(*block)] * 8
        + [vmem(*block)] * 5
        + [vmem(8, ROWS, COLS)] * 2
        + [
            vmem(2, 2, 2, 2, *slab),
            vmem(2, 2, 2, *slab), vmem(2, 2, 2, *slab),
            vmem(2, 2, *slab), vmem(2, 2, *slab),
            vmem(2, *slab), vmem(2, *slab),
            vmem(*slab), vmem(*slab),
            vmem(2, 2, 2, 2, *slab),
        ]
        + [
            pltpu.SemaphoreType.DMA((5,)),
            pltpu.SemaphoreType.DMA((6,)),
            pltpu.SemaphoreType.DMA((N_SEMS,)),
            pltpu.SemaphoreType.DMA((N_SEMS,)),
        ],
        compiler_params=pltpu.CompilerParams(
            collective_id=0, has_side_effects=True, vmem_limit_bytes=48 * 1024 * 1024
        ),
        name="window",
    )(
        before[0], now[0], after[0], adj[0], speed,
        src_pos[0], src_amp[0], rec_pos[0], observed[0], rate,
    )
    mid, last, adj_mid, adj_last, new, grad = outs
    return mid[None], last[None], adj_mid[None], adj_last[None], new.reshape(block), grad


def solution(mesh):
    wave = P("shot", None, "px", "py")
    group = P("shot", None, None)
    return jax.shard_map(
        local,
        mesh=mesh,
        in_specs=(wave, wave, wave, wave, P(None, "px", "py"), group, group, group, group, P()),
        out_specs=(wave, wave, wave, wave, P(None, "px", "py"), P("shot", "px", "py")),
        check_vma=False,
    )
```

time: 311 us -> 108 us (0.35)
  the two profiles are of different devices: /device:TPU:1 before, /device:TPU:40 now
where the time goes in v1:
time: 108 us
  Pallas kernels  95 us (88%)
  local copies, waits for them, and re-layouts  11.5 us (11%)
  between operations  1.32 us (1%)
    pallas_call x1, Pallas kernels, local(): pl.pallas_call(kernel, out_shape=[jax.ShapeDtypeStruct(block, f32)] * 4 +...  95 us
    unnamed x25, local copies, waits for them, and re-layouts  11.4 us

profile of v1, /device:TPU:40, one launch (start us, length us, event | category | flops | bytes accessed | tf_op | source)
XLA Modules:
  0.0 107.8 jit_solution(11024037243544103262)
XLA Ops:
  1.3 0.0 copy-start.8
  1.3 0.7 copy-done.8
  2.0 0.0 copy-start.7
  2.0 0.1 copy.18
  2.0 0.6 copy-done.7
  2.6 0.0 copy-start.5
  2.6 0.1 copy.16
  2.8 0.0 copy-start.6
  2.8 0.5 copy-done.5
  3.3 0.1 copy-done.6
  3.5 0.0 copy-start
  3.5 1.0 copy-done
  4.5 0.0 copy-start.1
  4.5 1.0 copy-done.1
  5.5 0.0 copy-start.2
  5.5 1.0 copy-done.2
  6.5 0.0 copy-start.3
  6.5 1.0 copy-done.3
  7.5 0.0 copy-start.4
  7.5 1.0 copy-done.4
  8.5 95.0 %window.1 = (f32[32,24,128]{2,1,0:T(8,128)S(1)}, f32[32,24,128]{2,1,0:T(8,128)S(1)}, f32[32,24,128]{2,1,0:T(8,128)S(1)}, f32[32,24,128]{2,1,0:T(8,128)S(1)}, f32...) custom-call(f32[32,24,128]{2,1,0:T(8,128)S(1)} %bitcast.14, f32[32,24,128]{2,1,0:T(8,128)S(1)} %bitcast.15, ...), custom_call_target="tpu_custom_call" | custom-call | tf_op jit(solution)/shard_map/window/pallas_call | solution.py:431
  103.5 0.7 copy.26
  104.2 0.7 copy.27
  105.0 0.7 copy.28
  105.7 0.7 copy.29
  106.5 0.7 copy.30
  107.2 0.6 copy.31
Async XLA Ops:
  1.3 0.7 copy-start.8
  2.0 0.7 copy-start.7
  2.6 0.7 copy-start.5
  2.8 0.7 copy-start.6
  3.5 1.0 copy-start
  4.5 1.0 copy-start.1
  5.5 1.0 copy-start.2
  6.5 1.0 copy-start.3
  7.5 1.0 copy-start.4

commit v2 on v1

--- a/solution.py
+++ b/solution.py
@@ -13,7 +13,7 @@
 NZ, ROWS, COLS = 32, 24, 128
 NREC, NSRC = 256, 8
 TILES = ROWS // 8
-UNROLL = 4
+UNROLL = 16
 
 (F_L, F_R, F_PL, F_PR, C_L, C_R, C_PL, C_PR, M_L, M_R, M_PL, M_PR, D_L, D_R, D_PL, D_PR) = range(16)
 SUM_A, SUM_B, SUM_C, SUM_D, ALL_D, ALL_C, ALL_B, ALL_A = range(16, 24)
@@ -21,14 +21,15 @@
 
 
 def kernel(
-    before_h, now_h, after_h, adj_h, speed_h, src_pos, src_amp, rec_pos, observed, rate,
-    mid_o, last_o, adj_mid_o, adj_last_o, new_o, grad_o,
+    before_h, now_h, after_h, adj_h, speed_h, src_pos_h, src_amp_h, rec_pos_h, observed_h, rate,
+    mid, last, amid, alast, new, grad,
     fnow, fmid, cadj, cmid,
-    before, after, adj, speed, lap1, last, amid, alast,
+    before, after, adj, speed, lap1,
+    src_pos, src_amp, rec_pos, observed,
     s_one, s_two, count, obs_two, obs_three,
     pack, halo,
-    term, ra, sa, rb, sb, rc, sc, rd, grad, new,
-    in_sem, out_sem, send_sem, recv_sem,
+    term, ra, sa, rb, sb, rc, sc, rd,
+    in_sem, send_sem, recv_sem,
 ):
     shot, px, py = lax.axis_index("shot"), lax.axis_index("px"), lax.axis_index("py")
     n_px, n_py = lax.axis_size("px"), lax.axis_size("py")
@@ -51,7 +52,13 @@
     load_speed = pltpu.make_async_copy(speed_h, speed, in_sem.at[2])
     load_before = pltpu.make_async_copy(before_h, before, in_sem.at[3])
     load_after = pltpu.make_async_copy(after_h, after, in_sem.at[4])
-    for load in (load_now, load_adj, load_speed, load_before, load_after):
+    load_small = [
+        pltpu.make_async_copy(source, target, in_sem.at[5 + k])
+        for k, (source, target) in enumerate(
+            ((src_pos_h, src_pos), (src_amp_h, src_amp), (rec_pos_h, rec_pos), (observed_h, observed))
+        )
+    ]
+    for load in (load_now, load_adj, load_speed, *load_small, load_before, load_after):
         load.start()
 
     barrier = pltpu.get_barrier_semaphore()
@@ -199,40 +206,43 @@
     halo_cadj.send_right()
     halo_cadj.send_lanes()
 
+    for load in load_small:
+        load.wait()
     first_start, second_start = px * ROWS, py * COLS
     place = lax.broadcasted_iota(jnp.int32, (8, COLS), 0) * COLS + lane
-    keys, amps = [], []
-    for j in range(NSRC):
-        first, second = src_pos[j, 1] - first_start, src_pos[j, 2] - second_start
-        owned = (first >= 0) & (first < ROWS) & (second >= 0) & (second < COLS)
-        keys.append(jnp.where(owned, (src_pos[j, 0] * ROWS + first) * COLS + second, -1))
-        amps.append((src_amp[0, j], src_amp[1, j]))
+    first, second = src_pos[1] - first_start, src_pos[2] - second_start
+    owned = (first >= 0) & (first < ROWS) & (second >= 0) & (second < COLS)
+    key = jnp.where(owned, (src_pos[0] * ROWS + first) * COLS + second, -1)
+
+    def spread(row, j):
+        return jnp.broadcast_to(row[:, j:j + 1], (8, COLS))
+
+    spikes = [(spread(key, j), spread(src_amp[0:1, :], j), spread(src_amp[1:2, :], j)) for j in range(NSRC)]
     for tile in range(TILES):
         rows = slice(8 * tile, 8 * tile + 8)
 
         def sources(z, _):
             here = place + (z * ROWS + 8 * tile) * COLS
             one, two = zero, zero
-            for key, (amp_one, amp_two) in zip(keys, amps):
-                hit = here == key
+            for cell, amp_one, amp_two in spikes:
+                hit = here == cell
                 one = one + jnp.where(hit, amp_one, 0.0)
                 two = two + jnp.where(hit, amp_two, 0.0)
             s_one[z, rows, :] = one
             s_two[z, rows, :] = two
             return 0
 
-        lax.fori_loop(0, NZ, sources, 0)
-
-    first = rec_pos[:, 1:2] - first_start
-    second = rec_pos[:, 2:3] - second_start
+        lax.fori_loop(0, NZ, sources, 0, unroll=4)
+
+    first = rec_pos[1] - first_start
     inside = (first >= 0) & (first < ROWS)
-    cell = jnp.where(inside, rec_pos[:, 0:1] * ROWS + first, -1).astype(jnp.float32)
-    cell_row = jnp.transpose(jnp.broadcast_to(cell, (NREC, COLS)))[0:1, :]
-    data = jnp.transpose(observed[...])
-    column = lax.broadcasted_iota(jnp.int32, (NREC, COLS), 1) == second
+    cell_row = jnp.where(inside, rec_pos[0] * ROWS + first, -1).astype(jnp.float32)
+    second = (rec_pos[2] - second_start).astype(jnp.float32)
+    data = jnp.transpose(jnp.concatenate([second, observed[...], jnp.zeros((5, NREC), jnp.float32)], axis=0))
+    column = lax.broadcasted_iota(jnp.int32, (NREC, COLS), 1).astype(jnp.float32) == data[:, 0:1]
     parts = [column.astype(jnp.float32).astype(jnp.bfloat16)]
     for k in range(2):
-        rest = jnp.where(column, jnp.broadcast_to(data[:, k:k + 1], (NREC, COLS)), 0.0)
+        rest = jnp.where(column, jnp.broadcast_to(data[:, k + 1:k + 2], (NREC, COLS)), 0.0)
         for _ in range(3):
             part = rest.astype(jnp.bfloat16)
             rest = rest - part.astype(jnp.float32)
@@ -263,6 +273,7 @@
             lap1[z, rows, :] = lap
             value = 2.0 * centre - before[z, rows, :] + coef_at(z, rows) * lap + s_one[z, rows, :]
             fmid[z + 4, ext, :] = value
+            mid[z, rows, :] = value
             return value
 
         over_depth(tile, 2, step)
@@ -275,8 +286,6 @@
     mid_tile(2)
     halo_mid.send_right()
     halo_mid.send_lanes()
-    store_mid = pltpu.make_async_copy(fmid.at[inner], mid_o, out_sem.at[0])
-    store_mid.start()
 
     load_after.wait()
     halo_cadj.wait_lanes()
@@ -330,10 +339,6 @@
     sum_a.start()
     halo_cmid.send_right()
     halo_cmid.send_lanes()
-    store_last = pltpu.make_async_copy(last, last_o, out_sem.at[1])
-    store_last.start()
-    store_amid = pltpu.make_async_copy(amid, adj_mid_o, out_sem.at[2])
-    store_amid.start()
 
     sum_a.wait_recv()
 
@@ -378,8 +383,6 @@
     total = sc[bit2] + rd[...]
     grad[...] = total
     new[bit2, bit1, bit0, core] = speed[pl.ds(2 * shot, 2)] - rate[0] * total
-    store_grad = pltpu.make_async_copy(grad, grad_o, out_sem.at[3])
-    store_grad.start()
 
     own = new.at[bit2, bit1, bit0, core]
     all_d = remote(own, own, ALL_D, near4)
@@ -401,19 +404,22 @@
     adj_tile(0)
     halo_cmid.wait_right()
     adj_tile(2)
-    store_alast = pltpu.make_async_copy(alast, adj_last_o, out_sem.at[4])
-    store_alast.start()
 
     all_a.wait_recv()
-    store_new = pltpu.make_async_copy(new, new_o, out_sem.at[5])
-    store_new.start()
 
     for field in (halo_now, halo_cadj, halo_mid, halo_cmid):
         field.finish()
     for copy in (sum_a, sum_b, sum_c, sum_d, all_d, all_c, all_b, all_a):
         copy.wait_send()
-    for store in (store_mid, store_last, store_amid, store_grad, store_alast, store_new):
-        store.wait()
+
+
+def write(*refs):
+    sem = refs[12]
+    copies = [pltpu.make_async_copy(refs[k], refs[6 + k], sem.at[k]) for k in range(6)]
+    for copy in copies:
+        copy.start()
+    for copy in copies:
+        copy.wait()
 
 
 def local(before, now, after, adj, speed, src_pos, src_amp, rec_pos, observed, rate):
@@ -425,17 +431,21 @@
     def vmem(*shape):
         return pltpu.VMEM(shape, f32)
 
-    anywhere = pl.BlockSpec(memory_space=pl.ANY)
+    in_hbm = pl.BlockSpec(memory_space=pltpu.HBM)
     in_vmem = pl.BlockSpec(memory_space=pltpu.VMEM)
     in_smem = pl.BlockSpec(memory_space=pltpu.SMEM)
     outs = pl.pallas_call(
         kernel,
         out_shape=[jax.ShapeDtypeStruct(block, f32)] * 4
         + [jax.ShapeDtypeStruct((2, 2, 2, 2) + slab, f32), jax.ShapeDtypeStruct(slab, f32)],
-        in_specs=[anywhere] * 5 + [in_smem, in_smem, in_vmem, in_vmem, in_smem],
-        out_specs=[anywhere] * 6,
+        in_specs=[in_hbm] * 9 + [in_smem],
+        out_specs=[in_vmem] * 6,
         scratch_shapes=[vmem(*padded)] * 4
-        + [vmem(*block)] * 8
+        + [vmem(*block)] * 5
+        + [
+            pltpu.VMEM((3, 1, NSRC), jnp.int32), vmem(2, NSRC),
+            pltpu.VMEM((3, 1, NREC), jnp.int32), vmem(2, NREC),
+        ]
         + [vmem(*block)] * 5
         + [vmem(8, ROWS, COLS)] * 2
         + [
@@ -443,24 +453,30 @@
             vmem(2, 2, 2, *slab), vmem(2, 2, 2, *slab),
             vmem(2, 2, *slab), vmem(2, 2, *slab),
             vmem(2, *slab), vmem(2, *slab),
-            vmem(*slab), vmem(*slab),
-            vmem(2, 2, 2, 2, *slab),
+            vmem(*slab),
         ]
         + [
-            pltpu.SemaphoreType.DMA((5,)),
-            pltpu.SemaphoreType.DMA((6,)),
+            pltpu.SemaphoreType.DMA((9,)),
             pltpu.SemaphoreType.DMA((N_SEMS,)),
             pltpu.SemaphoreType.DMA((N_SEMS,)),
         ],
         compiler_params=pltpu.CompilerParams(
-            collective_id=0, has_side_effects=True, vmem_limit_bytes=48 * 1024 * 1024
+            collective_id=0, has_side_effects=True, vmem_limit_bytes=53100 * 1024
         ),
         name="window",
     )(
         before[0], now[0], after[0], adj[0], speed,
-        src_pos[0], src_amp[0], rec_pos[0], observed[0], rate,
+        src_pos.transpose(2, 0, 1), src_amp[0], rec_pos.transpose(2, 0, 1), observed[0], rate,
     )
-    mid, last, adj_mid, adj_last, new, grad = outs
+    mid, last, adj_mid, adj_last, new, grad = pl.pallas_call(
+        write,
+        out_shape=[jax.ShapeDtypeStruct(out.shape, f32) for out in outs],
+        in_specs=[in_vmem] * 6,
+        out_specs=[in_hbm] * 6,
+        scratch_shapes=[pltpu.SemaphoreType.DMA((6,))],
+        compiler_params=pltpu.CompilerParams(vmem_limit_bytes=1024 * 1024),
+        name="write",
+    )(*outs)
     return mid[None], last[None], adj_mid[None], adj_last[None], new.reshape(block), grad
 
 

time: 108 us -> 93 us (0.86)
  local copies, waits for them, and re-layouts: 11.5 us -> 0.7 us
  Pallas kernels: 95 us -> 90.8 us
    unnamed x25 -> x8, local copies, waits for them, and re-layouts: 11.4 us -> 0.7 us
    pallas_call x1, Pallas kernels: 95 us -> 89.5 us  [local(): pl.pallas_call(kernel, out_shape=[jax.ShapeDtypeStruct(block, f32)] * 4 +...]
    pallas_call x0 -> x1, Pallas kernels: none -> 1.32 us  [local(): pl.pallas_call(write, out_shape=[jax.ShapeDtypeStruct(out.shape, f32) for...]
where the time goes in v2:
time: 93 us; the launch traced here: 92.8 us
  Pallas kernels  90.8 us (98%)
  between operations  1.32 us (1%)
    pallas_call x1, Pallas kernels, local(): pl.pallas_call(kernel, out_shape=[jax.ShapeDtypeStruct(block, f32)] * 4 +...  89.5 us

profile of v2, /device:TPU:40, one launch (start us, length us, event | category | flops | bytes accessed | tf_op | source)
XLA Modules:
  0.0 92.8 jit_solution(9477539567668094005)
XLA Ops:
  1.3 0.0 copy-start.2
  1.3 0.0 copy-start.3
  1.3 0.0 copy-start
  1.3 0.0 copy-start.1
  1.3 0.6 copy-done.2
  2.0 0.0 copy-done.3
  2.0 0.0 copy-done
  2.0 0.0 copy-done.1
  2.0 89.5 %window.1 = (f32[32,24,128]{2,1,0:T(8,128)S(1)}, f32[32,24,128]{2,1,0:T(8,128)S(1)}, f32[32,24,128]{2,1,0:T(8,128)S(1)}, f32[32,24,128]{2,1,0:T(8,128)S(1)}, f32...) custom-call(f32[32,24,128]{2,1,0:T(8,128)} %bitcast.17, f32[32,24,128]{2,1,0:T(8,128)} %bitcast.18, ...), custom_call_target="tpu_custom_call" | custom-call | tf_op jit(solution)/shard_map/window/pallas_call | solution.py:437
  91.5 1.3 %write.1 = (f32[32,24,128]{2,1,0:T(8,128)}, f32[32,24,128]{2,1,0:T(8,128)}, f32[32,24,128]{2,1,0:T(8,128)}, f32[32,24,128]{2,1,0:T(8,128)}, f32[2,2,2,2,2,24,128...) custom-call(f32[32,24,128]{2,1,0:T(8,128)S(1)} %get-tuple-element.18.refs_0_, f32[32,24,128]{2,1,0:T(8,128)S(1)} %get-tuple-element.19.refs_1_, ...), custom_call_target="tpu_custom_call" | custom-call | tf_op jit(solution)/shard_map/write/pallas_call | solution.py:471
Async XLA Ops:
  1.3 0.7 copy-start.2
  1.3 0.7 copy-start.3
  1.3 0.7 copy-start
  1.3 0.7 copy-start.1

commit v3 on v2

--- a/solution.py
+++ b/solution.py
@@ -16,8 +16,9 @@
 UNROLL = 16
 
 (F_L, F_R, F_PL, F_PR, C_L, C_R, C_PL, C_PR, M_L, M_R, M_PL, M_PR, D_L, D_R, D_PL, D_PR) = range(16)
-SUM_A, SUM_B, SUM_C, SUM_D, ALL_D, ALL_C, ALL_B, ALL_A = range(16, 24)
-N_SEMS = 24
+SUM_A, SUM_D, ALL_A = range(16, 19)
+SUM_B, ALL_B = 18, 21
+N_SEMS = 25
 
 
 def kernel(
@@ -28,7 +29,7 @@
     src_pos, src_amp, rec_pos, observed,
     s_one, s_two, count, obs_two, obs_three,
     pack, halo,
-    term, ra, sa, rb, sb, rc, sc, rd,
+    term, ra, sa, rb, sc, rd,
     in_sem, send_sem, recv_sem,
 ):
     shot, px, py = lax.axis_index("shot"), lax.axis_index("px"), lax.axis_index("py")
@@ -44,6 +45,7 @@
     mate = (shot + 1 - 2 * core, px, py)
     near1 = (shot + 2 * (1 - 2 * bit0), px, py)
     near2 = (shot + 4 * (1 - 2 * bit1), px, py)
+    near3 = (shot + 2 * (1 - 2 * bit0) + 4 * (1 - 2 * bit1), px, py)
     near4 = (shot + 8 * (1 - 2 * bit2), px, py)
 
     inner = (slice(4, 4 + NZ), slice(8, 8 + ROWS), slice(None))
@@ -62,7 +64,7 @@
         load.start()
 
     barrier = pltpu.get_barrier_semaphore()
-    partners = (left, right, prev, after_py, mate, near1, near2, near4)
+    partners = (left, right, prev, after_py, mate, near1, near2, near3, near4)
     for device in partners:
         pl.semaphore_signal(barrier, inc=1, device_id=device, device_id_type=MESH)
 
@@ -135,9 +137,16 @@
             pl.when(has_next)(self.to_prev.wait_recv)
             pl.when(has_prev)(self.to_next.wait_recv)
 
+        drained = False
+
+        def drain(self):
+            if not self.drained:
+                pl.when(has_left)(self.to_left.wait_send)
+                pl.when(has_right)(self.to_right.wait_send)
+            self.drained = True
+
         def finish(self):
-            pl.when(has_left)(self.to_left.wait_send)
-            pl.when(has_right)(self.to_right.wait_send)
+            self.drain()
             pl.when(has_prev)(self.to_prev.wait_send)
             pl.when(has_next)(self.to_next.wait_send)
 
@@ -202,8 +211,6 @@
             return value
 
         over_depth(tile, 1, scale)
-    halo_cadj.send_left()
-    halo_cadj.send_right()
     halo_cadj.send_lanes()
 
     for load in load_small:
@@ -261,6 +268,9 @@
         return 0
 
     lax.fori_loop(0, NZ // DEPTHS, receivers, 0)
+    halo_now.drain()
+    halo_cadj.send_left()
+    halo_cadj.send_right()
 
     load_before.wait()
     halo_now.wait_lanes()
@@ -349,14 +359,10 @@
         return 0
 
     lax.fori_loop(0, 4, add_a, 0)
-    sum_b = remote(sa.at[:, :, 1 - bit0], rb, SUM_B, near1)
-    sum_b.start()
-    sum_b.wait_recv()
-    for i in range(2):
-        for j in range(2):
-            sb[i, j] = sa[i, j, bit0] + rb[i, j]
-    sum_c = remote(sb.at[:, 1 - bit1], rc, SUM_C, near2)
-    sum_c.start()
+    others = ((3, near3, 1 - bit1, 1 - bit0), (2, near2, 1 - bit1, bit0), (1, near1, bit1, 1 - bit0))
+    sums = [remote(sa.at[:, i, j], rb.at[k - 1], SUM_B + k, device) for k, device, i, j in others]
+    for copy in sums:
+        copy.start()
 
     def adj_tile(tile):
         rows = slice(8 * tile, 8 * tile + 8)
@@ -374,42 +380,37 @@
     halo_cmid.wait_lanes()
     adj_tile(1)
 
-    sum_c.wait_recv()
+    for copy in sums:
+        copy.wait_recv()
     for i in range(2):
-        sc[i] = sb[i, bit1] + rc[i]
-    sum_d = remote(sc.at[1 - bit2], rd, SUM_D, near4)
+        sc[i] = sa[i, bit1, bit0] + rb[0, i] + rb[1, i] + rb[2, i]
+    sum_d = remote(sc, rd, SUM_D, near4)
     sum_d.start()
     sum_d.wait_recv()
-    total = sc[bit2] + rd[...]
-    grad[...] = total
-    new[bit2, bit1, bit0, core] = speed[pl.ds(2 * shot, 2)] - rate[0] * total
-
-    own = new.at[bit2, bit1, bit0, core]
-    all_d = remote(own, own, ALL_D, near4)
-    all_d.start()
-    all_d.wait_recv()
+    for i in range(2):
+        new[i, bit1, bit0, core] = speed[pl.ds(16 * i + 2 * lax.rem(shot, 8), 2)] - rate[0] * (sc[i] + rd[i])
+
     own = new.at[:, bit1, bit0, core]
-    all_c = remote(own, own, ALL_C, near2)
-    all_c.start()
-    all_c.wait_recv()
-    own = new.at[:, :, bit0, core]
-    all_b = remote(own, own, ALL_B, near1)
-    all_b.start()
-    all_b.wait_recv()
-    own = new.at[:, :, :, core]
-    all_a = remote(own, own, ALL_A, mate)
-    all_a.start()
-
+    gathers = [remote(own, own, ALL_B + k, device) for k, device, _, _ in others]
+    for copy in gathers:
+        copy.start()
+    grad[...] = sc[bit2] + rd[bit2]
     halo_cmid.wait_left()
     adj_tile(0)
     halo_cmid.wait_right()
     adj_tile(2)
+    for copy in gathers:
+        copy.wait_recv()
+    own = new.at[:, :, :, core]
+    all_a = remote(own, own, ALL_A, mate)
+    all_a.start()
+
 
     all_a.wait_recv()
 
     for field in (halo_now, halo_cadj, halo_mid, halo_cmid):
         field.finish()
-    for copy in (sum_a, sum_b, sum_c, sum_d, all_d, all_c, all_b, all_a):
+    for copy in (sum_a, *sums, sum_d, *gathers, all_a):
         copy.wait_send()
 
 
@@ -451,9 +452,8 @@
         + [
             vmem(2, 2, 2, 2, *slab),
             vmem(2, 2, 2, *slab), vmem(2, 2, 2, *slab),
-            vmem(2, 2, *slab), vmem(2, 2, *slab),
+            vmem(3, 2, *slab),
             vmem(2, *slab), vmem(2, *slab),
-            vmem(*slab),
         ]
         + [
             pltpu.SemaphoreType.DMA((9,)),

time: 93 us -> 87.3 us (0.939)
  the two profiles are of different devices: /device:TPU:40 before, /device:TPU:53 now
where the time goes in v3:
time: 87.3 us; the launch traced here: 87.1 us
  Pallas kernels  85.1 us (97%)
  between operations  1.32 us (2%)
    pallas_call x1, Pallas kernels, local(): pl.pallas_call(kernel, out_shape=[jax.ShapeDtypeStruct(block, f32)] * 4 +...  83.8 us

profile of v3, /device:TPU:53, one launch (start us, length us, event | category | flops | bytes accessed | tf_op | source)
XLA Modules:
  0.0 87.1 jit_solution(4834147181183311072)
XLA Ops:
  1.3 0.0 copy-start.2
  1.3 0.0 copy-start.3
  1.3 0.0 copy-start
  1.3 0.0 copy-start.1
  1.3 0.6 copy-done.2
  2.0 0.0 copy-done.3
  2.0 0.0 copy-done
  2.0 0.0 copy-done.1
  2.0 83.8 %window.1 = (f32[32,24,128]{2,1,0:T(8,128)S(1)}, f32[32,24,128]{2,1,0:T(8,128)S(1)}, f32[32,24,128]{2,1,0:T(8,128)S(1)}, f32[32,24,128]{2,1,0:T(8,128)S(1)}, f32...) custom-call(f32[32,24,128]{2,1,0:T(8,128)} %bitcast.17, f32[32,24,128]{2,1,0:T(8,128)} %bitcast.18, ...), custom_call_target="tpu_custom_call" | custom-call | tf_op jit(solution)/shard_map/window/pallas_call | solution.py:438
  85.8 1.3 %write.1 = (f32[32,24,128]{2,1,0:T(8,128)}, f32[32,24,128]{2,1,0:T(8,128)}, f32[32,24,128]{2,1,0:T(8,128)}, f32[32,24,128]{2,1,0:T(8,128)}, f32[2,2,2,2,2,24,128...) custom-call(f32[32,24,128]{2,1,0:T(8,128)S(1)} %get-tuple-element.18.refs_0_, f32[32,24,128]{2,1,0:T(8,128)S(1)} %get-tuple-element.19.refs_1_, ...), custom_call_target="tpu_custom_call" | custom-call | tf_op jit(solution)/shard_map/write/pallas_call | solution.py:471
Async XLA Ops:
  1.3 0.7 copy-start.2
  1.3 0.7 copy-start.3
  1.3 0.7 copy-start
  1.3 0.7 copy-start.1

commit v4 on v3

--- a/solution.py
+++ b/solution.py
@@ -68,36 +68,6 @@
     for device in partners:
         pl.semaphore_signal(barrier, inc=1, device_id=device, device_id_type=MESH)
 
-    for field in (fnow, fmid, cadj, cmid):
-        for plane in (0, 1, 2, 3, NZ + 4, NZ + 5, NZ + 6, NZ + 7):
-            field[plane] = jnp.zeros((ROWS + 16, COLS), jnp.float32)
-
-    @pl.when(px == 0)
-    def _():
-        def body(z, _):
-            for field in (fnow, fmid, cadj, cmid):
-                field[z + 4, 0:8, :] = jnp.zeros((8, COLS), jnp.float32)
-            return 0
-        lax.fori_loop(0, NZ, body, 0)
-
-    @pl.when(px == n_px - 1)
-    def _():
-        def body(z, _):
-            for field in (fnow, fmid, cadj, cmid):
-                field[z + 4, 8 + ROWS:16 + ROWS, :] = jnp.zeros((8, COLS), jnp.float32)
-            return 0
-        lax.fori_loop(0, NZ, body, 0)
-
-    @pl.when(py == 0)
-    def _():
-        for k in range(4):
-            halo[2 * k] = jnp.zeros((ROWS, COLS), jnp.float32)
-
-    @pl.when(py == n_py - 1)
-    def _():
-        for k in range(4):
-            halo[2 * k + 1] = jnp.zeros((ROWS, COLS), jnp.float32)
-
     lane = lax.broadcasted_iota(jnp.int32, (8, COLS), 1)
     group = lane // 4
 
@@ -191,6 +161,37 @@
     pl.semaphore_wait(barrier, len(partners))
     halo_now.send_left()
     halo_now.send_right()
+
+    for field in (fnow, fmid, cadj, cmid):
+        for plane in (0, 1, 2, 3, NZ + 4, NZ + 5, NZ + 6, NZ + 7):
+            field[plane] = jnp.zeros((ROWS + 16, COLS), jnp.float32)
+
+    @pl.when(px == 0)
+    def _():
+        def body(z, _):
+            for field in (fnow, fmid, cadj, cmid):
+                field[z + 4, 0:8, :] = jnp.zeros((8, COLS), jnp.float32)
+            return 0
+        lax.fori_loop(0, NZ, body, 0)
+
+    @pl.when(px == n_px - 1)
+    def _():
+        def body(z, _):
+            for field in (fnow, fmid, cadj, cmid):
+                field[z + 4, 8 + ROWS:16 + ROWS, :] = jnp.zeros((8, COLS), jnp.float32)
+            return 0
+        lax.fori_loop(0, NZ, body, 0)
+
+    @pl.when(py == 0)
+    def _():
+        for k in range(4):
+            halo[2 * k] = jnp.zeros((ROWS, COLS), jnp.float32)
+
+    @pl.when(py == n_py - 1)
+    def _():
+        for k in range(4):
+            halo[2 * k + 1] = jnp.zeros((ROWS, COLS), jnp.float32)
+
     for tile in range(TILES):
         over_depth(tile, 0, lambda z: fnow[z + 4, 8 + 8 * tile:16 + 8 * tile, :])
     halo_now.send_lanes()

time: 87.3 us -> 87.7 us (level)
  the two profiles are of different devices: /device:TPU:53 before, /device:TPU:43 now
where the time goes in v4:
time: 87.7 us; the launch traced here: 87.5 us
  Pallas kernels  85.5 us (97%)
  between operations  1.32 us (2%)
    pallas_call x1, Pallas kernels, local(): pl.pallas_call(kernel, out_shape=[jax.ShapeDtypeStruct(block, f32)] * 4 +...  84.1 us

profile of v4, /device:TPU:43, one launch (start us, length us, event | category | flops | bytes accessed | tf_op | source)
XLA Modules:
  0.0 87.5 jit_solution(169711780862389149)
XLA Ops:
  1.3 0.0 copy-start.2
  1.3 0.0 copy-start.3
  1.3 0.0 copy-start
  1.3 0.0 copy-start.1
  1.3 0.6 copy-done.2
  2.0 0.0 copy-done.3
  2.0 0.0 copy-done
  2.0 0.0 copy-done.1
  2.0 84.1 %window.1 = (f32[32,24,128]{2,1,0:T(8,128)S(1)}, f32[32,24,128]{2,1,0:T(8,128)S(1)}, f32[32,24,128]{2,1,0:T(8,128)S(1)}, f32[32,24,128]{2,1,0:T(8,128)S(1)}, f32...) custom-call(f32[32,24,128]{2,1,0:T(8,128)} %bitcast.17, f32[32,24,128]{2,1,0:T(8,128)} %bitcast.18, ...), custom_call_target="tpu_custom_call" | custom-call | tf_op jit(solution)/shard_map/window/pallas_call | solution.py:439
  86.2 1.3 %write.1 = (f32[32,24,128]{2,1,0:T(8,128)}, f32[32,24,128]{2,1,0:T(8,128)}, f32[32,24,128]{2,1,0:T(8,128)}, f32[32,24,128]{2,1,0:T(8,128)}, f32[2,2,2,2,2,24,128...) custom-call(f32[32,24,128]{2,1,0:T(8,128)S(1)} %get-tuple-element.18.refs_0_, f32[32,24,128]{2,1,0:T(8,128)S(1)} %get-tuple-element.19.refs_1_, ...), custom_call_target="tpu_custom_call" | custom-call | tf_op jit(solution)/shard_map/write/pallas_call | solution.py:472
Async XLA Ops:
  1.3 0.7 copy-start.2
  1.3 0.7 copy-start.3
  1.3 0.7 copy-start
  1.3 0.7 copy-start.1
